TPU v7x, 128 devices: a whole 4x4x4 slice. The times are simulated.
128 devices in a mesh: expert: 16 (over x, y), etp: 2 (over core), dp: 4 (over z).
Axes of the slice: x: 4, y: 4, z: 4, core: 2. Of those that a mesh axis runs over, the one named last changes fastest.
Arguments:
- frames: bfloat16 [24576, 1024], P(('expert', 'dp'), 'etp'), may hold values from -6 to 6
- out_grad: bfloat16 [24576, 1024], P(('expert', 'dp'), 'etp'), may hold values from -6 to 6
- routes: int32 [24576, 2], P(('expert', 'dp')), may hold values from 0 to 31, all different within a row; in each aligned block of 384 rows (0 to 383, 384 to 767, ...) at most 48 rows name the same one
- gate_levels: int32 [24576, 2], P(('expert', 'dp')), may hold values from 16 to 255
- w_gate: bfloat16 [32, 1024, 2048], P('expert', None, 'etp'), may hold values from -0.1875 to 0.1875
- w_up: bfloat16 [32, 1024, 2048], P('expert', None, 'etp'), may hold values from -0.1875 to 0.1875
- w_down: bfloat16 [32, 1024, 2048], P('expert', None, 'etp'), may hold values from -0.125 to 0.125
Outputs:
- frame_grad: bfloat16 [24576, 1024], P(('expert', 'dp'), 'etp')
- gate_wgrad: bfloat16 [32, 1024, 2048], P('expert', 'dp', 'etp')
- up_wgrad: bfloat16 [32, 1024, 2048], P('expert', 'dp', 'etp')
- down_wgrad: bfloat16 [32, 1024, 2048], P('expert', 'dp', 'etp')
Inputs may be any that keep to these rules, and one draw needn't show every extreme that they name: `routes`: within the 384 frames of one device, no expert is named more than 48 times over both columns, and in every draw some expert is named exactly 48 times there; the two choices of a frame differ.
All inputs are finite; a program needn't handle non-finite values.
Results may differ from a plain program's by a relative error of at most 0.014.
Values may be sent and summed in bfloat16 or wider, within the bound.
A program may use at most 128 MiB of HBM per device.

v0:
```python
import jax
import jax.numpy as jnp
from jax import lax
from jax.experimental import pallas as pl
from jax.experimental.pallas import tpu as pltpu
from jax.sharding import PartitionSpec as P

MESH = pl.DeviceIdType.MESH
BF, F32 = jnp.bfloat16, jnp.float32
PEERS, DP = 16, 4
EXPERTS = 32
CAP = 48
TOK = 384
D = 1024
HALF = 512
FF = 1024
ROWS = 2 * PEERS * CAP
CH = 256
NCH = FF // CH
SL = D // DP
RB = 384
ANY = pl.BlockSpec(memory_space=pl.ANY)
VM = pl.BlockSpec(memory_space=pltpu.VMEM)
ORDER = (
    (1, 0), (0, 2), (3, 1), (2, 3), (0, 1), (2, 0), (1, 3), (3, 2),
    (0, 3), (1, 1), (2, 2), (3, 0), (1, 2), (2, 1), (3, 3),
)


def pack_kernel(routes_ref, levels_ref, frames_ref, grads_ref, out_ref):
    ids = lax.broadcasted_iota(jnp.int32, (EXPERTS, TOK), 0)
    first = ids == routes_ref[0:1, :]
    second = ids == routes_ref[1:2, :]
    named = first | second
    before = lax.broadcasted_iota(jnp.int32, (TOK, TOK), 0) < lax.broadcasted_iota(
        jnp.int32, (TOK, TOK), 1
    )
    count = jnp.dot(
        named.astype(F32).astype(BF), before.astype(F32).astype(BF), preferred_element_type=F32
    ).astype(jnp.int32)
    place = jnp.where(named, count, -1)
    level = jnp.where(first, levels_ref[0:1, :], levels_ref[1:2, :])
    gate = level.astype(F32) / 256.0
    step = 8
    for group in range(EXPERTS // step):
        here = place[group * step : (group + 1) * step]
        slots = lax.broadcasted_iota(jnp.int32, (step, CAP, TOK), 1)
        hit = here[:, None, :] == slots
        pick = jnp.where(hit, 1.0, 0.0).reshape(step * CAP, TOK).astype(BF)
        scaled = (
            jnp.where(hit, gate[group * step : (group + 1) * step][:, None, :], 0.0)
            .reshape(step * CAP, TOK)
            .astype(BF)
        )
        rows = pl.ds(group * step * CAP, step * CAP)
        out_ref[rows, 0:HALF] = jnp.dot(
            pick, frames_ref[...], preferred_element_type=F32
        ).astype(BF)
        out_ref[rows, HALF : 2 * HALF] = jnp.dot(
            scaled, grads_ref[...], preferred_element_type=F32
        ).astype(BF)


def unpack_kernel(routes_ref, back_ref, out_ref):
    ids = lax.broadcasted_iota(jnp.int32, (TOK, EXPERTS), 1)
    first = ids == routes_ref[:, 0:1]
    second = ids == routes_ref[:, 1:2]
    named = (first | second).astype(F32).astype(BF)
    before = lax.broadcasted_iota(jnp.int32, (TOK, TOK), 1) < lax.broadcasted_iota(
        jnp.int32, (TOK, TOK), 0
    )
    count = jnp.dot(before.astype(F32).astype(BF), named, preferred_element_type=F32)
    slot = count + (ids * CAP).astype(F32)
    slot0 = jnp.sum(jnp.where(first, slot, 0.0), axis=1, keepdims=True).astype(jnp.int32)
    slot1 = jnp.sum(jnp.where(second, slot, 0.0), axis=1, keepdims=True).astype(jnp.int32)
    lanes = lax.broadcasted_iota(jnp.int32, (TOK, EXPERTS * CAP), 1)
    pick = jnp.where((lanes == slot0) | (lanes == slot1), 1.0, 0.0).astype(BF)
    out_ref[...] = jnp.dot(pick, back_ref[...], preferred_element_type=F32).astype(BF)


def layer_kernel(
    send_ref, wg_hbm, wu_hbm, wd_hbm,
    og_ref, ou_ref, od_ref, back_ref,
    recv, wts, turned, acts, sendp, recvp, kept, own_half, sib_send, sib_recv, ret, outs, outq,
    w_sem, loc_sem, d_send, d_recv, s_send, s_recv, p_send, p_recv,
    h_send, h_recv, r_send, r_recv, rl_sem, q_send, q_recv, o_sem,
):
    e = lax.axis_index("expert")
    c = lax.axis_index("etp")
    z = lax.axis_index("dp")
    ex, ey = e // 4, lax.rem(e, 4)
    p = z + 1 - 2 * lax.rem(z, 2)
    q = 3 - z
    o = 3 - p
    own = z // 2
    out_refs = (og_ref, ou_ref, od_ref)

    wcopy = [
        pltpu.make_async_copy(w.at[own], wts.at[i], w_sem.at[i])
        for i, w in enumerate((wg_hbm, wu_hbm, wd_hbm))
    ]
    for w in wcopy:
        w.start()

    def at(dx, dy):
        ax = jnp.where(c == 1, dy, dx)
        ay = jnp.where(c == 1, dx, dy)
        return lax.rem(ex + ax, 4) * 4 + lax.rem(ey + ay, 4)

    barrier = pltpu.get_barrier_semaphore()

    def greet(i, _):
        d = lax.rem(e + i, PEERS)
        pl.semaphore_signal(barrier, inc=1, device_id=(d, c, q), device_id_type=MESH)

        @pl.when(i > 0)
        def _():
            pl.semaphore_signal(barrier, inc=1, device_id=(d, c, z), device_id_type=MESH)

        return 0

    lax.fori_loop(0, PEERS, greet, 0)
    pl.semaphore_signal(barrier, inc=1, device_id=(e, c, p), device_id_type=MESH)
    pl.semaphore_signal(barrier, inc=1, device_id=(e, 1 - c, z), device_id_type=MESH)
    pl.semaphore_wait(barrier, 2 * PEERS + 1)

    plane = (z, q)

    def rows_of(k, s):
        return pl.ds(pl.multiple_of((k * PEERS + s) * CAP, CAP), CAP)

    def give(d, k):
        return pltpu.make_async_remote_copy(
            src_ref=send_ref.at[d, own if k == 0 else 1 - own],
            dst_ref=recv.at[c, rows_of(k, e)],
            send_sem=d_send.at[k, d],
            recv_sem=d_recv.at[k, e],
            device_id=(d, c, plane[k]),
            device_id_type=MESH,
        )

    def take(s, k):
        return pltpu.make_async_remote_copy(
            src_ref=recv.at[c, rows_of(k, s)],
            dst_ref=recv.at[c, rows_of(k, s)],
            send_sem=d_send.at[k, s],
            recv_sem=d_recv.at[k, s],
            device_id=(s, c, plane[k]),
            device_id_type=MESH,
        )

    def share(half, s, k):
        return pltpu.make_async_remote_copy(
            src_ref=recv.at[half, rows_of(k, s)],
            dst_ref=recv.at[half, rows_of(k, s)],
            send_sem=s_send.at[k, s],
            recv_sem=s_recv.at[k, s],
            device_id=(e, 1 - c, z),
            device_id_type=MESH,
        )

    local = pltpu.make_async_copy(send_ref.at[e, own], recv.at[c, rows_of(0, e)], loc_sem)
    local.start()
    for k in range(2):
        for off in ORDER:
            give(at(*off), k).start()
        if k == 1:
            give(e, 1).start()
    for w in wcopy:
        w.wait()
    local.wait()
    share(c, e, 0).start()

    def arrive(k):
        for dx, dy in ORDER:
            s = at((4 - dx) % 4, (4 - dy) % 4)
            take(s, k).wait_recv()
            share(c, s, k).start()
        if k == 1:
            take(e, 1).wait_recv()
            share(c, e, 1).start()

        def mate(s, _):
            share(1 - c, s, k).wait_recv()
            return 0

        lax.fori_loop(0, PEERS, mate, 0)

    def forward(k, j, ch):
        rows = pl.ds(pl.multiple_of(k * (ROWS // 2) + j * RB, RB), RB)
        cols = pl.ds(pl.multiple_of(ch * CH, CH), CH)

        def product(i, base):
            total = jnp.dot(
                recv[0, rows, base : base + HALF], wts[i, 0:HALF, cols], preferred_element_type=F32
            )
            return total + jnp.dot(
                recv[1, rows, base : base + HALF], wts[i, HALF:D, cols], preferred_element_type=F32
            )

        pre_gate = product(0, 0)
        pre_up = product(1, 0)
        sig = jax.nn.sigmoid(pre_gate)
        act = pre_gate * sig
        acts[2, ch, rows, :] = (act * pre_up).astype(BF)
        grad = product(2, HALF)
        acts[0, ch, rows, :] = (
            grad * pre_up * sig * (1.0 + pre_gate * (1.0 - sig))
        ).astype(BF)
        acts[1, ch, rows, :] = (grad * act).astype(BF)

    def turn(k):
        def body(i, _):
            half, j = i // 2, lax.rem(i, 2)
            rows = pl.ds(pl.multiple_of(k * (ROWS // 2) + j * RB, RB), RB)
            for t in range(2):
                for h in range(2):
                    base = t * HALF + h * SL
                    block = recv[half, rows, base : base + SL]
                    turned[t, 2 * half + h, :, rows] = block.T
            return 0

        lax.fori_loop(0, 4, body, 0)

    arrive(0)
    turn(0)

    def early(i, _):
        forward(0, lax.rem(i, 2), i // 2)
        return 0

    lax.fori_loop(0, 2 * NCH, early, 0)
    arrive(1)
    turn(1)

    def to_mate(ch, m):
        return pltpu.make_async_remote_copy(
            src_ref=sendp.at[ch, m],
            dst_ref=recvp.at[ch, m],
            send_sem=p_send.at[ch, m],
            recv_sem=p_recv.at[ch, m],
            device_id=(e, c, p),
            device_id_type=MESH,
        )

    def weight_grad(m, ch, part):
        lhs = turned[0 if m < 2 else 1, part]
        return jnp.dot(lhs, acts[m, ch], preferred_element_type=F32)

    def late(ch, _):
        for j in range(2):
            forward(1, j, ch)
        for m in range(3):
            sendp[ch, m, 0] = weight_grad(m, ch, p).astype(BF)
            sendp[ch, m, 1] = weight_grad(m, ch, o).astype(BF)
            to_mate(ch, m).start()
        return 0

    lax.fori_loop(0, NCH, late, 0)

    def swap(b):
        return pltpu.make_async_remote_copy(
            src_ref=sib_send.at[b],
            dst_ref=sib_recv.at[b],
            send_sem=h_send.at[b],
            recv_sem=h_recv.at[b],
            device_id=(e, 1 - c, z),
            device_id_type=MESH,
        )

    def input_grad(i, _):
        b = lax.rem(i + 2, 4)
        rows = pl.ds(pl.multiple_of(b * RB, RB), RB)

        def half_of(h):
            feats = pl.ds(pl.multiple_of(h * HALF, HALF), HALF)
            total = jnp.zeros((RB, HALF), F32)
            for w in range(2):
                for ch in range(NCH):
                    total += lax.dot_general(
                        acts[w, ch, rows, :],
                        wts[w, feats, ch * CH : (ch + 1) * CH],
                        (((1,), (1,)), ((), ())),
                        preferred_element_type=F32,
                    )
            return total

        sib_send[b] = half_of(1 - c).astype(BF)
        swap(b).start()
        own_half[b] = half_of(c)
        return 0

    lax.fori_loop(0, 4, input_grad, 0)

    def keep(ch, _):
        for m in range(3):
            kept[ch, m, 0] = weight_grad(m, ch, z)
            kept[ch, m, 1] = weight_grad(m, ch, q)
        return 0

    lax.fori_loop(0, NCH, keep, 0)

    def give_back(s, k):
        return pltpu.make_async_remote_copy(
            src_ref=ret.at[rows_of(k, s)],
            dst_ref=back_ref.at[e, own],
            send_sem=r_send.at[k, s],
            recv_sem=r_recv.at[k, e],
            device_id=(s, c, plane[k]),
            device_id_type=MESH,
        )

    def take_back(s, k):
        return pltpu.make_async_remote_copy(
            src_ref=ret.at[rows_of(k, s)],
            dst_ref=back_ref.at[s, own if k == 0 else 1 - own],
            send_sem=r_send.at[k, s],
            recv_sem=r_recv.at[k, s],
            device_id=(s, c, plane[k]),
            device_id_type=MESH,
        )

    back_local = pltpu.make_async_copy(ret.at[rows_of(0, e)], back_ref.at[e, own], rl_sem)
    for b in (2, 3, 0, 1):
        swap(b).wait_recv()
        ret[pl.ds(b * RB, RB), :] = (own_half[b] + sib_recv[b].astype(F32)).astype(BF)
        if b == 3:
            for off in ORDER:
                give_back(at(*off), 1).start()
            give_back(e, 1).start()
        if b == 1:
            for off in ORDER:
                give_back(at(*off), 0).start()
            back_local.start()

    def to_q(ch, m):
        place = out_refs[m].at[own, :, pl.ds(pl.multiple_of(ch * CH, CH), CH)]
        return pltpu.make_async_remote_copy(
            src_ref=outq.at[ch, m],
            dst_ref=place,
            send_sem=q_send.at[ch, m],
            recv_sem=q_recv.at[ch, m],
            device_id=(e, c, q),
            device_id_type=MESH,
        )

    def from_q(ch, m):
        place = out_refs[m].at[1 - own, :, pl.ds(pl.multiple_of(ch * CH, CH), CH)]
        return pltpu.make_async_remote_copy(
            src_ref=outq.at[ch, m],
            dst_ref=place,
            send_sem=q_send.at[ch, m],
            recv_sem=q_recv.at[ch, m],
            device_id=(e, c, q),
            device_id_type=MESH,
        )

    def to_out(ch, m):
        place = out_refs[m].at[own, :, pl.ds(pl.multiple_of(ch * CH, CH), CH)]
        return pltpu.make_async_copy(outs.at[ch, m], place, o_sem.at[ch, m])

    def finish(ch, _):
        for m in range(3):
            to_mate(ch, m).wait_recv()
            outq[ch, m] = (kept[ch, m, 1] + recvp[ch, m, 1].astype(F32)).astype(BF)
            to_q(ch, m).start()
            outs[ch, m] = (kept[ch, m, 0] + recvp[ch, m, 0].astype(F32)).astype(BF)
            to_out(ch, m).start()
        return 0

    lax.fori_loop(0, NCH, finish, 0)

    def drain_peers(i, _):
        d = lax.rem(e + i, PEERS)
        give(d, 1).wait_send()
        share(c, d, 0).wait_send()
        share(c, d, 1).wait_send()
        give_back(d, 1).wait_send()
        take_back(d, 1).wait_recv()

        @pl.when(i > 0)
        def _():
            give(d, 0).wait_send()
            give_back(d, 0).wait_send()
            take_back(d, 0).wait_recv()

        return 0

    lax.fori_loop(0, PEERS, drain_peers, 0)
    back_local.wait()

    def drain(ch, _):
        swap(ch).wait_send()
        for m in range(3):
            to_mate(ch, m).wait_send()
            to_q(ch, m).wait_send()
            from_q(ch, m).wait_recv()
            to_out(ch, m).wait()
        return 0

    lax.fori_loop(0, NCH, drain, 0)


def layer(send, w_gate, w_up, w_down):
    dma = pltpu.SemaphoreType.DMA
    grad = jax.ShapeDtypeStruct((2, SL, FF), BF)
    return pl.pallas_call(
        layer_kernel,
        out_shape=[grad, grad, grad, jax.ShapeDtypeStruct((PEERS, 2, CAP, HALF), BF)],
        in_specs=[ANY] * 4,
        out_specs=[ANY] * 4,
        scratch_shapes=[
            pltpu.VMEM((2, ROWS, 2 * HALF), BF),
            pltpu.VMEM((3, D, FF), BF),
            pltpu.VMEM((2, DP, SL, ROWS), BF),
            pltpu.VMEM((3, NCH, ROWS, CH), BF),
            pltpu.VMEM((NCH, 3, 2, SL, CH), BF),
            pltpu.VMEM((NCH, 3, 2, SL, CH), BF),
            pltpu.VMEM((NCH, 3, 2, SL, CH), F32),
            pltpu.VMEM((4, RB, HALF), F32),
            pltpu.VMEM((4, RB, HALF), BF),
            pltpu.VMEM((4, RB, HALF), BF),
            pltpu.VMEM((ROWS, HALF), BF),
            pltpu.VMEM((NCH, 3, SL, CH), BF),
            pltpu.VMEM((NCH, 3, SL, CH), BF),
            dma((3,)),
            dma,
            dma((2, PEERS)),
            dma((2, PEERS)),
            dma((2, PEERS)),
            dma((2, PEERS)),
            dma((NCH, 3)),
            dma((NCH, 3)),
            dma((4,)),
            dma((4,)),
            dma((2, PEERS)),
            dma((2, PEERS)),
            dma,
            dma((NCH, 3)),
            dma((NCH, 3)),
            dma((NCH, 3)),
        ],
        compiler_params=pltpu.CompilerParams(
            collective_id=1, has_side_effects=True, vmem_limit_bytes=60 * 1024 * 1024
        ),
        cost_estimate=pl.CostEstimate(
            flops=16 * ROWS * D * FF, bytes_accessed=20_000_000, transcendentals=ROWS * FF
        ),
        name="layer",
    )(send, w_gate, w_up, w_down)


def local(frames, out_grad, routes, gate_levels, w_gate, w_up, w_down):
    send = pl.pallas_call(
        pack_kernel,
        out_shape=jax.ShapeDtypeStruct((EXPERTS * CAP, 2 * HALF), BF),
        in_specs=[VM] * 4,
        out_specs=VM,
        name="pack",
    )(routes.T, gate_levels.T, frames, out_grad)
    send = send.reshape(PEERS, 2, CAP, 2 * HALF)
    gate_grad, up_grad, down_grad, back = layer(send, w_gate, w_up, w_down)
    frame_grad = pl.pallas_call(
        unpack_kernel,
        out_shape=jax.ShapeDtypeStruct((TOK, HALF), BF),
        in_specs=[VM] * 2,
        out_specs=VM,
        name="unpack",
    )(routes, back.reshape(EXPERTS * CAP, HALF))
    return frame_grad, gate_grad, up_grad, down_grad


def solution(mesh):
    placed = (
        P(("expert", "dp"), "etp"),
        P(("expert", "dp"), "etp"),
        P(("expert", "dp"), None),
        P(("expert", "dp"), None),
        P("expert", None, "etp"),
        P("expert", None, "etp"),
        P("expert", None, "etp"),
    )
    return jax.shard_map(
        local,
        mesh=mesh,
        in_specs=placed,
        out_specs=(
            P(("expert", "dp"), "etp"),
            P("expert", "dp", "etp"),
            P("expert", "dp", "etp"),
            P("expert", "dp", "etp"),
        ),
        check_vma=False,
    )
```

profile of v0, /device:TPU:1, one launch (start us, length us, event | category | flops | bytes accessed | tf_op | source)
XLA Modules:
  0.0 156.9 jit_solution(9712429709858826724)
XLA Ops:
  0.6 4.7 %pack.1 = bf16[1536,1024]{1,0:T(8,128)(2,1)} custom-call(s32[2,384]{1,0:T(2,128)} %bitcast.6, s32[2,384]{1,0:T(2,128)} %bitcast.7, bf16[384,512]{1,0:T(8,128)(2,1)} %frames_ref.1, bf16[384,512]{1,0:T(8,128)(2,1)} %grads_ref.1), custom_call_target="tpu_custom_call" | custom-call | tf_op jit(solution)/shard_map/pack/pallas_call | solution.py:454
  5.4 0.0 copy-start.2
  5.4 142.9 %layer.1 = (bf16[2,256,1024]{2,1,0:T(8,128)(2,1)}, bf16[2,256,1024]{2,1,0:T(8,128)(2,1)}, bf16[2,256,1024]{2,1,0:T(8,128)(2,1)}, bf16[16,2,48,512]{3,2,1,0:T(8,128)(2,1)}) custom-call(bf16[16,2,48,1024]{3,2,1,0:T(8,128)(2,1)} %bitcast.4, bf16[2,1024,1024]{2,1,0:T(8,128)(2,1)} %wg_hbm.1, bf16[2,1024,1024]{2,1,0:T(8,128)(2,1)} %wu_hbm.1, ...), custom_call_target="tpu_custom_call" | custom-call | flops 25769803776 | bytes 20000000 | tf_op jit(solution)/shard_map/layer/pallas_call | solution.py:407
  148.3 0.0 copy-start.1
  148.3 0.0 copy-start
  148.3 0.0 copy-done.2
  148.3 0.8 copy.11.routes_ref
  149.2 3.5 %unpack.1 = bf16[384,512]{1,0:T(8,128)(2,1)} custom-call(s32[384,2]{1,0:T(8,128)} %copy.11.routes_ref, bf16[1536,512]{1,0:T(8,128)(2,1)} %bitcast.5), custom_call_target="tpu_custom_call" | custom-call | tf_op jit(solution)/shard_map/unpack/pallas_call | solution.py:463
  152.7 2.3 %copy.15 = bf16[2,256,1024]{2,1,0:T(8,128)(2,1)} copy(bf16[2,256,1024]{2,1,0:T(8,128)(2,1)} %get-tuple-element.17) | data formatting | bytes 2097152
  154.9 0.0 copy-done.1
  154.9 1.0 copy.16
  155.9 0.0 copy-done
  155.9 1.0 copy.17
Async XLA Ops:
  5.4 143.0 %copy-start.2 = (s32[384,2]{0,1:T(2,128)S(1)}, s32[384,2]{0,1:T(2,128)}, u32[]{:S(2)}) copy-start(s32[384,2]{0,1:T(2,128)} %param.9) | copy-start | bytes 9220
  148.3 6.6 %copy-start.1 = (bf16[2,256,1024]{2,1,0:T(8,128)(2,1)S(1)}, bf16[2,256,1024]{2,1,0:T(8,128)(2,1)}, u32[]{:S(2)}) copy-start(bf16[2,256,1024]{2,1,0:T(8,128)(2,1)} %get-tuple-element.18) | copy-start | bytes 3145732
  148.3 7.6 %copy-start = (bf16[2,256,1024]{2,1,0:T(8,128)(2,1)S(1)}, bf16[2,256,1024]{2,1,0:T(8,128)(2,1)}, u32[]{:S(2)}) copy-start(bf16[2,256,1024]{2,1,0:T(8,128)(2,1)} %get-tuple-element.19) | copy-start | bytes 3145732
where the time goes:
time: 157 us
  Pallas kernels  151 us (96%)
  local copies, waits for them, and re-layouts  5.04 us (3%)
    pallas_call x1, Pallas kernels, layer(): pl.pallas_call(layer_kernel, out_shape=[grad, grad, grad, jax.ShapeDtypeS...  143 us
    unnamed x10, local copies, waits for them, and re-layouts  5.04 us
    pallas_call x1, Pallas kernels, local(): pl.pallas_call(pack_kernel, out_shape=jax.ShapeDtypeStruct((EXPERTS * CAP...  4.72 us
    pallas_call x1, Pallas kernels, local(): pl.pallas_call(unpack_kernel, out_shape=jax.ShapeDtypeStruct((TOK, HALF),...  3.51 us

commit v1 on v0

v1 whole, which is shorter than its diff:
```python
import jax
import jax.numpy as jnp
from jax import lax
from jax.experimental import pallas as pl
from jax.experimental.pallas import tpu as pltpu
from jax.sharding import PartitionSpec as P

MESH = pl.DeviceIdType.MESH
BF, F32 = jnp.bfloat16, jnp.float32
PEERS, DP = 16, 4
EXPERTS = 32
CAP = 48
TOK = 384
D = 1024
HALF = 512
FF = 1024
ROWS = 2 * PEERS * CAP
CH = 256
NCH = FF // CH
SL = D // DP
RB = 384
ANY = pl.BlockSpec(memory_space=pl.ANY)
VM = pl.BlockSpec(memory_space=pltpu.VMEM)


def offsets(names):
    kinds = {
        "a": [(1, 0), (3, 0)], "b": [(0, 1), (0, 3)], "c": [(1, 1), (3, 3)], "d": [(1, 3), (3, 1)],
        "e": [(2, 1), (2, 3)], "f": [(1, 2), (3, 2)], "g": [(2, 0)], "h": [(0, 2)], "i": [(2, 2)],
        "l": [(0, 0)],
    }
    return [off for name in names for off in kinds[name]]


def mirrored(off):
    return (4 - off[0]) % 4, (4 - off[1]) % 4


GROUPS = [
    (offsets(here), offsets(there))
    for here, there in zip(("lid", "af", "be", "cgh"), ("be", "dil", "cgh", "af"))
]
BLOCKS = [
    block for here, there in GROUPS for a, b in zip(here, there) for block in (a + (0,), b + (1,))
]
INDEX = {block: i for i, block in enumerate(BLOCKS)}
NBLOCK = len(BLOCKS)
SENDS = [
    BLOCKS,
    [
        block
        for here, there in GROUPS
        for a, b in zip(here, there)
        for block in (mirrored(b) + (1,), mirrored(a) + (0,))
    ],
]
GROUP = NBLOCK // 4


def layer_kernel(
    routes_ref, levels_ref, frames_ref, grads_ref, wg_hbm, wu_hbm, wd_hbm,
    og_ref, ou_ref, od_ref, frame_ref,
    place_ref, gate_ref, pick_ref, scaled_ref, send_ref, recv, wts, turned, acts,
    sendp, recvp, own_half, sib_send, sib_recv, ret, back, outs, outq, frame_out,
    w_sem, loc_sem, d_send, d_recv, s_send, s_recv, p_send, p_recv,
    h_send, h_recv, r_send, r_recv, rl_sem, q_send, q_recv, o_sem, f_sem,
):
    e = lax.axis_index("expert")
    c = lax.axis_index("etp")
    z = lax.axis_index("dp")
    ex, ey = e // 4, lax.rem(e, 4)
    p = z + 1 - 2 * lax.rem(z, 2)
    q = 3 - z
    o = 3 - p
    own = z // 2
    plane = (z, q)
    out_refs = (og_ref, ou_ref, od_ref)

    barrier = pltpu.get_barrier_semaphore()

    def greet(i, _):
        d = lax.rem(e + i, PEERS)
        pl.semaphore_signal(barrier, inc=1, device_id=(d, c, q), device_id_type=MESH)

        @pl.when(i > 0)
        def _():
            pl.semaphore_signal(barrier, inc=1, device_id=(d, c, z), device_id_type=MESH)

        return 0

    lax.fori_loop(0, PEERS, greet, 0)
    pl.semaphore_signal(barrier, inc=1, device_id=(e, c, p), device_id_type=MESH)
    pl.semaphore_signal(barrier, inc=1, device_id=(e, 1 - c, z), device_id_type=MESH)

    wcopy = [
        pltpu.make_async_copy(w.at[own], wts.at[i], w_sem.at[i])
        for i, w in enumerate((wg_hbm, wu_hbm, wd_hbm))
    ]
    for w in wcopy:
        w.start()

    ids = lax.broadcasted_iota(jnp.int32, (EXPERTS, TOK), 0)
    first = ids == routes_ref[0:1, :]
    second = ids == routes_ref[1:2, :]
    named = first | second
    before = lax.broadcasted_iota(jnp.int32, (TOK, TOK), 0) < lax.broadcasted_iota(
        jnp.int32, (TOK, TOK), 1
    )
    count = jnp.dot(
        named.astype(F32).astype(BF), before.astype(F32).astype(BF), preferred_element_type=F32
    )
    place_ref[...] = jnp.where(named, count, -1.0)
    level = jnp.where(first, levels_ref[0:1, :], levels_ref[1:2, :])
    gate_ref[...] = level.astype(F32) / 256.0
    slots = lax.broadcasted_iota(jnp.int32, (CAP, TOK), 0).astype(F32)

    def at(dx, dy):
        return lax.rem(ex + dx, 4) * 4 + lax.rem(ey + dy, 4)

    def rows_of(i):
        return pl.ds(i * CAP if isinstance(i, int) else pl.multiple_of(i * CAP, CAP), CAP)

    def group_rows(g):
        return pl.ds(g * RB if isinstance(g, int) else pl.multiple_of(g * RB, RB), RB)

    def pack(g):
        for j in range(GROUP):
            dx, dy, k = BLOCKS[g * GROUP + j]
            expert = 2 * at(dx, dy) + (own if k == 0 else 1 - own)
            hit = place_ref[pl.ds(expert, 1), :] == slots
            pick_ref[rows_of(j), :] = jnp.where(hit, 1.0, 0.0).astype(BF)
            scaled_ref[rows_of(j), :] = jnp.where(hit, gate_ref[pl.ds(expert, 1), :], 0.0).astype(BF)
        rows = group_rows(g)
        send_ref[rows, 0:HALF] = jnp.dot(
            pick_ref[...], frames_ref[...], preferred_element_type=F32
        ).astype(BF)
        send_ref[rows, HALF : 2 * HALF] = jnp.dot(
            scaled_ref[...], grads_ref[...], preferred_element_type=F32
        ).astype(BF)

    def choose(a, b):
        return a if a == b else jnp.where(c == 0, a, b)

    def give(t):
        one, two = SENDS[0][t], SENDS[1][t]
        dx, dy, k, i = [
            choose(a, b) for a, b in zip(one + (INDEX[one],), two + (INDEX[two],))
        ]
        return pltpu.make_async_remote_copy(
            src_ref=send_ref.at[rows_of(i)],
            dst_ref=recv.at[c, rows_of(i)],
            send_sem=d_send.at[i],
            recv_sem=d_recv.at[i],
            device_id=(at(dx, dy), c, jnp.where(k == 0, z, q)),
            device_id_type=MESH,
        )

    def take(i):
        return pltpu.make_async_remote_copy(
            src_ref=send_ref.at[rows_of(i)],
            dst_ref=recv.at[c, rows_of(i)],
            send_sem=d_send.at[i],
            recv_sem=d_recv.at[i],
            device_id=(e, c, q),
            device_id_type=MESH,
        )

    def share(half, i):
        return pltpu.make_async_remote_copy(
            src_ref=recv.at[half, rows_of(i)],
            dst_ref=recv.at[half, rows_of(i)],
            send_sem=s_send.at[i],
            recv_sem=s_recv.at[i],
            device_id=(e, 1 - c, z),
            device_id_type=MESH,
        )

    local = pltpu.make_async_copy(send_ref.at[rows_of(0)], recv.at[c, rows_of(0)], loc_sem)
    for g in range(4):
        pack(g)
        if g == 0:
            pl.semaphore_wait(barrier, 2 * PEERS + 1)
            local.start()
        for t in range(g * GROUP, (g + 1) * GROUP):
            if SENDS[0][t] == (0, 0, 0):
                pl.when(c == 1)(lambda t=t: give(t).start())
            elif SENDS[1][t] == (0, 0, 0):
                pl.when(c == 0)(lambda t=t: give(t).start())
            else:
                give(t).start()
    for w in wcopy:
        w.wait()

    def arrive(g):
        for i in range(g * GROUP, (g + 1) * GROUP):
            if i == 0:
                local.wait()
            else:
                take(i).wait_recv()
            share(c, i).start()

        def mate(j, _):
            share(1 - c, g * GROUP + j).wait_recv()
            return 0

        lax.fori_loop(0, GROUP, mate, 0)

    def forward(g, ch):
        rows = group_rows(g)
        cols = pl.ds(pl.multiple_of(ch * CH, CH), CH)

        def product(i, base):
            total = jnp.dot(
                recv[0, rows, base : base + HALF], wts[i, 0:HALF, cols], preferred_element_type=F32
            )
            return total + jnp.dot(
                recv[1, rows, base : base + HALF], wts[i, HALF:D, cols], preferred_element_type=F32
            )

        pre_gate = product(0, 0)
        pre_up = product(1, 0)
        sig = jax.nn.sigmoid(pre_gate)
        act = pre_gate * sig
        acts[2, ch, rows, :] = (act * pre_up).astype(BF)
        grad = product(2, HALF)
        acts[0, ch, rows, :] = (
            grad * pre_up * sig * (1.0 + pre_gate * (1.0 - sig))
        ).astype(BF)
        acts[1, ch, rows, :] = (grad * act).astype(BF)

    def turn(g):
        rows = group_rows(g)

        def body(half, _):
            for t in range(2):
                for h in range(2):
                    base = t * HALF + h * SL
                    turned[t, 2 * half + h, :, rows] = recv[half, rows, base : base + SL].T
            return 0

        lax.fori_loop(0, 2, body, 0)

    def early(i, _):
        forward(i // NCH, lax.rem(i, NCH))
        return 0

    for g in range(4):
        arrive(g)
        turn(g)
        if g < 2:
            lax.fori_loop(g * NCH, (g + 1) * NCH, early, 0)

    def to_mate(ch, m, i):
        return pltpu.make_async_remote_copy(
            src_ref=sendp.at[i, ch, m],
            dst_ref=recvp.at[i, ch, m],
            send_sem=p_send.at[i, ch, m],
            recv_sem=p_recv.at[i, ch, m],
            device_id=(e, c, p),
            device_id_type=MESH,
        )

    def weight_grad(m, ch, part):
        lhs = turned[0 if m < 2 else 1, part]
        return jnp.dot(lhs, acts[m, ch], preferred_element_type=F32)

    def beyond(ch, _):
        def rest(g, _):
            forward(g, ch)
            return 0

        lax.fori_loop(2, 4, rest, 0)
        for m in range(3):
            sendp[0, ch, m] = weight_grad(m, ch, o).astype(BF)
            to_mate(ch, m, 0).start()
        return 0

    lax.fori_loop(0, NCH, beyond, 0)

    def swap(b):
        return pltpu.make_async_remote_copy(
            src_ref=sib_send.at[b],
            dst_ref=sib_recv.at[b],
            send_sem=h_send.at[b],
            recv_sem=h_recv.at[b],
            device_id=(e, 1 - c, z),
            device_id_type=MESH,
        )

    def input_grad(b, _):
        rows = group_rows(b)

        def half_of(h):
            feats = pl.ds(pl.multiple_of(h * HALF, HALF), HALF)
            total = jnp.zeros((RB, HALF), F32)
            for w in range(2):
                for ch in range(NCH):
                    total += lax.dot_general(
                        acts[w, ch, rows, :],
                        wts[w, feats, ch * CH : (ch + 1) * CH],
                        (((1,), (1,)), ((), ())),
                        preferred_element_type=F32,
                    )
            return total

        sib_send[b] = half_of(1 - c).astype(BF)
        swap(b).start()
        own_half[b] = half_of(c)
        return 0

    lax.fori_loop(0, 4, input_grad, 0)

    def ending(ch, _):
        for m in range(3):
            sendp[1, ch, m] = weight_grad(m, ch, p).astype(BF)
            to_mate(ch, m, 1).start()
        return 0

    lax.fori_loop(0, NCH, ending, 0)

    def give_back(i):
        dx, dy, k = BLOCKS[i]
        return pltpu.make_async_remote_copy(
            src_ref=ret.at[rows_of(i)],
            dst_ref=back.at[e, own],
            send_sem=r_send.at[i],
            recv_sem=r_recv.at[k, e],
            device_id=(at((4 - dx) % 4, (4 - dy) % 4), c, plane[k]),
            device_id_type=MESH,
        )

    def take_back(s, k):
        return pltpu.make_async_remote_copy(
            src_ref=ret.at[rows_of(0)],
            dst_ref=back.at[s, own if k == 0 else 1 - own],
            send_sem=r_send.at[0],
            recv_sem=r_recv.at[k, s],
            device_id=(s, c, plane[k]),
            device_id_type=MESH,
        )

    back_local = pltpu.make_async_copy(ret.at[rows_of(0)], back.at[e, own], rl_sem)
    for b in range(4):
        swap(b).wait_recv()
        ret[group_rows(b), :] = (own_half[b] + sib_recv[b].astype(F32)).astype(BF)
        for i in range(b * GROUP, (b + 1) * GROUP):
            if i == 0:
                back_local.start()
            else:
                give_back(i).start()

    def place_of(ch, m, expert):
        return out_refs[m].at[expert, :, pl.ds(pl.multiple_of(ch * CH, CH), CH)]

    def with_q(ch, m, expert):
        return pltpu.make_async_remote_copy(
            src_ref=outq.at[ch, m],
            dst_ref=place_of(ch, m, expert),
            send_sem=q_send.at[ch, m],
            recv_sem=q_recv.at[ch, m],
            device_id=(e, c, q),
            device_id_type=MESH,
        )

    def to_out(ch, m):
        return pltpu.make_async_copy(outs.at[ch, m], place_of(ch, m, own), o_sem.at[ch, m])

    def pass_on(ch, _):
        for m in range(3):
            total = weight_grad(m, ch, q)
            to_mate(ch, m, 0).wait_recv()
            outq[ch, m] = (total + recvp[0, ch, m].astype(F32)).astype(BF)
            with_q(ch, m, own).start()
        return 0

    lax.fori_loop(0, NCH, pass_on, 0)

    def finish(ch, _):
        for m in range(3):
            total = weight_grad(m, ch, z)
            to_mate(ch, m, 1).wait_recv()
            outs[ch, m] = (total + recvp[1, ch, m].astype(F32)).astype(BF)
            to_out(ch, m).start()
        return 0

    lax.fori_loop(0, NCH // 2, finish, 0)

    def drain_back(i, _):
        take_back(i, 1).wait_recv()

        @pl.when(i != e)
        def _():
            take_back(i, 0).wait_recv()

        return 0

    lax.fori_loop(0, PEERS, drain_back, 0)
    back_local.wait()
    total = jnp.zeros((TOK, HALF), F32)
    step = 8
    for g in range(EXPERTS // step):
        parts = []
        for j in range(step):
            x = g * step + j
            parts.append(jnp.where(place_ref[x : x + 1, :] == slots, 1.0, 0.0).astype(BF))
        pick = jnp.concatenate(parts, axis=0)
        rows = back[g * step // 2 : (g + 1) * step // 2].reshape(step * CAP, HALF)
        total += jnp.dot(pick.T, rows, preferred_element_type=F32)
    frame_out[...] = total.astype(BF)
    frame_copy = pltpu.make_async_copy(frame_out, frame_ref, f_sem)
    frame_copy.start()

    lax.fori_loop(NCH // 2, NCH, finish, 0)

    def drain_blocks(i, _):
        share(c, i).wait_send()

        @pl.when(i > 0)
        def _():
            take(i).wait_send()
            pltpu.make_async_remote_copy(
                src_ref=ret.at[rows_of(i)],
                dst_ref=back.at[e, own],
                send_sem=r_send.at[i],
                recv_sem=r_recv.at[0, e],
                device_id=(e, c, q),
                device_id_type=MESH,
            ).wait_send()

        return 0

    lax.fori_loop(0, NBLOCK, drain_blocks, 0)
    frame_copy.wait()

    def drain(ch, _):
        swap(ch).wait_send()
        for m in range(3):
            for i in range(2):
                to_mate(ch, m, i).wait_send()
            with_q(ch, m, own).wait_send()
            with_q(ch, m, 1 - own).wait_recv()
            to_out(ch, m).wait()
        return 0

    lax.fori_loop(0, NCH, drain, 0)


def layer(routes, levels, frames, out_grad, w_gate, w_up, w_down):
    dma = pltpu.SemaphoreType.DMA
    grad = jax.ShapeDtypeStruct((2, SL, FF), BF)
    return pl.pallas_call(
        layer_kernel,
        out_shape=[grad, grad, grad, jax.ShapeDtypeStruct((TOK, HALF), BF)],
        in_specs=[VM] * 4 + [ANY] * 3,
        out_specs=[ANY] * 4,
        scratch_shapes=[
            pltpu.VMEM((EXPERTS, TOK), F32),
            pltpu.VMEM((EXPERTS, TOK), F32),
            pltpu.VMEM((RB, TOK), BF),
            pltpu.VMEM((RB, TOK), BF),
            pltpu.VMEM((ROWS, 2 * HALF), BF),
            pltpu.VMEM((2, ROWS, 2 * HALF), BF),
            pltpu.VMEM((3, D, FF), BF),
            pltpu.VMEM((2, DP, SL, ROWS), BF),
            pltpu.VMEM((3, NCH, ROWS, CH), BF),
            pltpu.VMEM((2, NCH, 3, SL, CH), BF),
            pltpu.VMEM((2, NCH, 3, SL, CH), BF),
            pltpu.VMEM((4, RB, HALF), F32),
            pltpu.VMEM((4, RB, HALF), BF),
            pltpu.VMEM((4, RB, HALF), BF),
            pltpu.VMEM((ROWS, HALF), BF),
            pltpu.VMEM((PEERS, 2, CAP, HALF), BF),
            pltpu.VMEM((NCH, 3, SL, CH), BF),
            pltpu.VMEM((NCH, 3, SL, CH), BF),
            pltpu.VMEM((TOK, HALF), BF),
            dma((3,)),
            dma,
            dma((NBLOCK,)),
            dma((NBLOCK,)),
            dma((NBLOCK,)),
            dma((NBLOCK,)),
            dma((2, NCH, 3)),
            dma((2, NCH, 3)),
            dma((4,)),
            dma((4,)),
            dma((NBLOCK,)),
            dma((2, PEERS)),
            dma,
            dma((NCH, 3)),
            dma((NCH, 3)),
            dma((NCH, 3)),
            dma,
        ],
        compiler_params=pltpu.CompilerParams(
            collective_id=1, has_side_effects=True, vmem_limit_bytes=60 * 1024 * 1024
        ),
        cost_estimate=pl.CostEstimate(
            flops=16 * ROWS * D * FF, bytes_accessed=20_000_000, transcendentals=ROWS * FF
        ),
        name="layer",
    )(routes, levels, frames, out_grad, w_gate, w_up, w_down)


def settle_kernel(*refs):
    n = (len(refs) - 2) // 3
    ins, outs, held = refs[:n], refs[n : 2 * n], refs[2 * n : 3 * n]
    in_sem, out_sem = refs[3 * n :]
    pieces = []
    for i in range(n):
        half = ins[i].shape[0] // 2
        for j in range(2):
            part = pl.ds(j * half, half)
            pieces.append(
                (
                    pltpu.make_async_copy(ins[i].at[part], held[i].at[part], in_sem.at[i, j]),
                    pltpu.make_async_copy(held[i].at[part], outs[i].at[part], out_sem.at[i, j]),
                )
            )
    for load, _ in pieces:
        load.start()
    for load, store in pieces:
        load.wait()
        store.start()
    for _, store in pieces:
        store.wait()


def settle(*arrays):
    n = len(arrays)
    return pl.pallas_call(
        settle_kernel,
        out_shape=[jax.ShapeDtypeStruct(a.shape, a.dtype) for a in arrays],
        in_specs=[ANY] * n,
        out_specs=[ANY] * n,
        scratch_shapes=[pltpu.VMEM(a.shape, a.dtype) for a in arrays]
        + [pltpu.SemaphoreType.DMA((n, 2))] * 2,
        name="settle",
    )(*arrays)


def local(frames, out_grad, routes, gate_levels, w_gate, w_up, w_down):
    gate_grad, up_grad, down_grad, frame_grad = settle(
        *layer(routes.T, gate_levels.T, frames, out_grad, w_gate, w_up, w_down)
    )
    return frame_grad, gate_grad, up_grad, down_grad


def solution(mesh):
    placed = (
        P(("expert", "dp"), "etp"),
        P(("expert", "dp"), "etp"),
        P(("expert", "dp"), None),
        P(("expert", "dp"), None),
        P("expert", None, "etp"),
        P("expert", None, "etp"),
        P("expert", None, "etp"),
    )
    return jax.shard_map(
        local,
        mesh=mesh,
        in_specs=placed,
        out_specs=(
            P(("expert", "dp"), "etp"),
            P("expert", "dp", "etp"),
            P("expert", "dp", "etp"),
            P("expert", "dp", "etp"),
        ),
        check_vma=False,
    )
```

time: 157 us -> 139 us (0.89)
  Pallas kernels: 151 us -> 138 us
  local copies, waits for them, and re-layouts: 5.04 us -> 0 us
    pallas_call x1, Pallas kernels: 143 us -> 135 us  [layer(): pl.pallas_call(layer_kernel, out_shape=[grad, grad, grad, jax.ShapeDtypeS...]
    pallas_call x2 -> x1, Pallas kernels: 8.23 us -> 2.96 us  [settle(): pl.pallas_call(settle_kernel, out_shape=[jax.ShapeDtypeStruct(a.shape, a....]
    unnamed x10 -> x0, local copies, waits for them, and re-layouts: 5.04 us -> none
where the time goes in v1:
time: 139 us; the launch traced here: 138 us
  Pallas kernels  138 us (99%)
    pallas_call x1, Pallas kernels, layer(): pl.pallas_call(layer_kernel, out_shape=[grad, grad, grad, jax.ShapeDtypeS...  135 us
    pallas_call x1, Pallas kernels, settle(): pl.pallas_call(settle_kernel, out_shape=[jax.ShapeDtypeStruct(a.shape, a....  2.96 us

profile of v1, /device:TPU:1, one launch (start us, length us, event | category | flops | bytes accessed | tf_op | source)
XLA Modules:
  0.0 138.4 jit_solution(15176827321986634483)
XLA Ops:
  0.6 134.8 %layer.1 = (bf16[2,256,1024]{2,1,0:T(8,128)(2,1)}, bf16[2,256,1024]{2,1,0:T(8,128)(2,1)}, bf16[2,256,1024]{2,1,0:T(8,128)(2,1)}, bf16[384,512]{1,0:T(8,128)(2,1)}) custom-call(s32[2,384]{1,0:T(2,128)} %bitcast.2, s32[2,384]{1,0:T(2,128)} %bitcast.3, bf16[384,512]{1,0:T(8,128)(2,1)} %frames_ref.1, bf16[384,512]{1,0:T(8,128)(2,1)} %grads_ref.1, ...), custom_call_target="tpu_custom_call" | custom-call | flops 25769803776 | bytes 20000000 | tf_op jit(solution)/shard_map/layer/pallas_call | solution.py:451
  135.5 3.0 %settle.1 = (bf16[2,256,1024]{2,1,0:T(8,128)(2,1)}, bf16[2,256,1024]{2,1,0:T(8,128)(2,1)}, bf16[2,256,1024]{2,1,0:T(8,128)(2,1)}, bf16[384,512]{1,0:T(8,128)(2,1)}) custom-call(bf16[2,256,1024]{2,1,0:T(8,128)(2,1)} %get-tuple-element.12.refs_0_, bf16[2,256,1024]{2,1,0:T(8,128)(2,1)} %get-tuple-element.13.refs_1_, ...), custom_call_target="tpu_custom_call" | custom-call | tf_op jit(solution)/shard_map/settle/pallas_call | solution.py:530

commit v2 on v1

--- a/solution.py
+++ b/solution.py
@@ -20,7 +20,6 @@
 SL = D // DP
 RB = 384
 ANY = pl.BlockSpec(memory_space=pl.ANY)
-VM = pl.BlockSpec(memory_space=pltpu.VMEM)
 
 
 def offsets(names):
@@ -58,11 +57,12 @@
 
 
 def layer_kernel(
-    routes_ref, levels_ref, frames_ref, grads_ref, wg_hbm, wu_hbm, wd_hbm,
+    routes_hbm, levels_hbm, frames_hbm, grads_hbm, wg_hbm, wu_hbm, wd_hbm,
     og_ref, ou_ref, od_ref, frame_ref,
+    routes_ref, levels_ref, frames_ref, grads_ref,
     place_ref, gate_ref, pick_ref, scaled_ref, send_ref, recv, wts, turned, acts,
     sendp, recvp, own_half, sib_send, sib_recv, ret, back, outs, outq, frame_out,
-    w_sem, loc_sem, d_send, d_recv, s_send, s_recv, p_send, p_recv,
+    i_sem, w_sem, loc_sem, d_send, d_recv, s_send, s_recv, p_send, p_recv,
     h_send, h_recv, r_send, r_recv, rl_sem, q_send, q_recv, o_sem, f_sem,
 ):
     e = lax.axis_index("expert")
@@ -76,6 +76,19 @@
     plane = (z, q)
     out_refs = (og_ref, ou_ref, od_ref)
 
+    loads = [
+        pltpu.make_async_copy(source, target, i_sem.at[i])
+        for i, (source, target) in enumerate(
+            (
+                (routes_hbm, routes_ref),
+                (levels_hbm, levels_ref),
+                (frames_hbm, frames_ref),
+                (grads_hbm, grads_ref),
+            )
+        )
+    ]
+    for load in loads:
+        load.start()
     barrier = pltpu.get_barrier_semaphore()
 
     def greet(i, _):
@@ -98,6 +111,9 @@
     ]
     for w in wcopy:
         w.start()
+
+    for load in loads:
+        load.wait()
 
     ids = lax.broadcasted_iota(jnp.int32, (EXPERTS, TOK), 0)
     first = ids == routes_ref[0:1, :]
@@ -247,7 +263,7 @@
     for g in range(4):
         arrive(g)
         turn(g)
-        if g < 2:
+        if g < 3:
             lax.fori_loop(g * NCH, (g + 1) * NCH, early, 0)
 
     def to_mate(ch, m, i):
@@ -269,7 +285,7 @@
             forward(g, ch)
             return 0
 
-        lax.fori_loop(2, 4, rest, 0)
+        lax.fori_loop(3, 4, rest, 0)
         for m in range(3):
             sendp[0, ch, m] = weight_grad(m, ch, o).astype(BF)
             to_mate(ch, m, 0).start()
@@ -316,7 +332,6 @@
             to_mate(ch, m, 1).start()
         return 0
 
-    lax.fori_loop(0, NCH, ending, 0)
 
     def give_back(i):
         dx, dy, k = BLOCKS[i]
@@ -348,6 +363,8 @@
                 back_local.start()
             else:
                 give_back(i).start()
+
+    lax.fori_loop(0, NCH, ending, 0)
 
     def place_of(ch, m, expert):
         return out_refs[m].at[expert, :, pl.ds(pl.multiple_of(ch * CH, CH), CH)]
@@ -451,9 +468,13 @@
     return pl.pallas_call(
         layer_kernel,
         out_shape=[grad, grad, grad, jax.ShapeDtypeStruct((TOK, HALF), BF)],
-        in_specs=[VM] * 4 + [ANY] * 3,
+        in_specs=[ANY] * 7,
         out_specs=[ANY] * 4,
         scratch_shapes=[
+            pltpu.VMEM((2, TOK), jnp.int32),
+            pltpu.VMEM((2, TOK), jnp.int32),
+            pltpu.VMEM((TOK, HALF), BF),
+            pltpu.VMEM((TOK, HALF), BF),
             pltpu.VMEM((EXPERTS, TOK), F32),
             pltpu.VMEM((EXPERTS, TOK), F32),
             pltpu.VMEM((RB, TOK), BF),
@@ -473,6 +494,7 @@
             pltpu.VMEM((NCH, 3, SL, CH), BF),
             pltpu.VMEM((NCH, 3, SL, CH), BF),
             pltpu.VMEM((TOK, HALF), BF),
+            dma((4,)),
             dma((3,)),
             dma,
             dma((NBLOCK,)),

time: 139 us -> 129 us (0.928)
  Pallas kernels: 138 us -> 129 us
    pallas_call x1, Pallas kernels: 135 us -> 126 us  [layer(): pl.pallas_call(layer_kernel, out_shape=[grad, grad, grad, jax.ShapeDtypeS...]
where the time goes in v2:
time: 129 us
  Pallas kernels  129 us (100%)
    pallas_call x1, Pallas kernels, layer(): pl.pallas_call(layer_kernel, out_shape=[grad, grad, grad, jax.ShapeDtypeS...  126 us
    pallas_call x1, Pallas kernels, settle(): pl.pallas_call(settle_kernel, out_shape=[jax.ShapeDtypeStruct(a.shape, a....  2.96 us

profile of v2, /device:TPU:1, one launch (start us, length us, event | category | flops | bytes accessed | tf_op | source)
XLA Modules:
  0.0 129.2 jit_solution(10269935958502167578)
XLA Ops:
  0.6 125.6 %layer.1 = (bf16[2,256,1024]{2,1,0:T(8,128)(2,1)}, bf16[2,256,1024]{2,1,0:T(8,128)(2,1)}, bf16[2,256,1024]{2,1,0:T(8,128)(2,1)}, bf16[384,512]{1,0:T(8,128)(2,1)}) custom-call(s32[2,384]{1,0:T(2,128)} %bitcast.2, s32[2,384]{1,0:T(2,128)} %bitcast.3, bf16[384,512]{1,0:T(8,128)(2,1)} %frames_hbm.1, bf16[384,512]{1,0:T(8,128)(2,1)} %grads_hbm.1, ...), custom_call_target="tpu_custom_call" | custom-call | flops 25769803776 | bytes 20000000 | tf_op jit(solution)/shard_map/layer/pallas_call | solution.py:468
  126.2 3.0 %settle.1 = (bf16[2,256,1024]{2,1,0:T(8,128)(2,1)}, bf16[2,256,1024]{2,1,0:T(8,128)(2,1)}, bf16[2,256,1024]{2,1,0:T(8,128)(2,1)}, bf16[384,512]{1,0:T(8,128)(2,1)}) custom-call(bf16[2,256,1024]{2,1,0:T(8,128)(2,1)} %get-tuple-element.12.refs_0_, bf16[2,256,1024]{2,1,0:T(8,128)(2,1)} %get-tuple-element.13.refs_1_, ...), custom_call_target="tpu_custom_call" | custom-call | tf_op jit(solution)/shard_map/settle/pallas_call | solution.py:552

commit v3 on v2

--- a/solution.py
+++ b/solution.py
@@ -54,6 +54,7 @@
     ],
 ]
 GROUP = NBLOCK // 4
+DETOURS = (NCH, 0)
 
 
 def layer_kernel(
@@ -61,18 +62,20 @@
     og_ref, ou_ref, od_ref, frame_ref,
     routes_ref, levels_ref, frames_ref, grads_ref,
     place_ref, gate_ref, pick_ref, scaled_ref, send_ref, recv, wts, turned, acts,
-    sendp, recvp, own_half, sib_send, sib_recv, ret, back, outs, outq, frame_out,
-    i_sem, w_sem, loc_sem, d_send, d_recv, s_send, s_recv, p_send, p_recv,
+    sendp, recvp, passing, own_half, sib_send, sib_recv, ret, back, outs, outq, frame_out,
+    i_sem, w_sem, loc_sem, d_send, d_recv, s_send, s_recv, p_send, p_recv, n_send, n_recv,
     h_send, h_recv, r_send, r_recv, rl_sem, q_send, q_recv, o_sem, f_sem,
 ):
     e = lax.axis_index("expert")
     c = lax.axis_index("etp")
     z = lax.axis_index("dp")
     ex, ey = e // 4, lax.rem(e, 4)
-    p = z + 1 - 2 * lax.rem(z, 2)
-    q = 3 - z
-    o = 3 - p
-    own = z // 2
+    odd = lax.rem(ex + ey, 2) == 1
+    low, high = z + 1 - 2 * lax.rem(z, 2), 3 - z
+    p, q = jnp.where(odd, high, low), jnp.where(odd, low, high)
+    o = lax.rem(z + 2, 4)
+    here, there = z // 2, lax.rem((z + 1) // 2, 2)
+    own, own_flip = jnp.where(odd, there, here), jnp.where(odd, here, there)
     plane = (z, q)
     out_refs = (og_ref, ou_ref, od_ref)
 
@@ -91,6 +94,9 @@
         load.start()
     barrier = pltpu.get_barrier_semaphore()
 
+    def at(dx, dy):
+        return lax.rem(ex + dx, 4) * 4 + lax.rem(ey + dy, 4)
+
     def greet(i, _):
         d = lax.rem(e + i, PEERS)
         pl.semaphore_signal(barrier, inc=1, device_id=(d, c, q), device_id_type=MESH)
@@ -102,6 +108,12 @@
         return 0
 
     lax.fori_loop(0, PEERS, greet, 0)
+    for dx in range(4):
+        for dy in range(4):
+            if (dx + dy) % 2 == 1:
+                pl.semaphore_signal(
+                    barrier, inc=1, device_id=(at(dx, dy), c, p), device_id_type=MESH
+                )
     pl.semaphore_signal(barrier, inc=1, device_id=(e, c, p), device_id_type=MESH)
     pl.semaphore_signal(barrier, inc=1, device_id=(e, 1 - c, z), device_id_type=MESH)
 
@@ -130,9 +142,6 @@
     gate_ref[...] = level.astype(F32) / 256.0
     slots = lax.broadcasted_iota(jnp.int32, (CAP, TOK), 0).astype(F32)
 
-    def at(dx, dy):
-        return lax.rem(ex + dx, 4) * 4 + lax.rem(ey + dy, 4)
-
     def rows_of(i):
         return pl.ds(i * CAP if isinstance(i, int) else pl.multiple_of(i * CAP, CAP), CAP)
 
@@ -142,7 +151,8 @@
     def pack(g):
         for j in range(GROUP):
             dx, dy, k = BLOCKS[g * GROUP + j]
-            expert = 2 * at(dx, dy) + (own if k == 0 else 1 - own)
+            theirs = own_flip if (dx + dy) % 2 else own
+            expert = 2 * at(dx, dy) + (theirs if k == 0 else 1 - theirs)
             hit = place_ref[pl.ds(expert, 1), :] == slots
             pick_ref[rows_of(j), :] = jnp.where(hit, 1.0, 0.0).astype(BF)
             scaled_ref[rows_of(j), :] = jnp.where(hit, gate_ref[pl.ds(expert, 1), :], 0.0).astype(BF)
@@ -159,15 +169,17 @@
 
     def give(t):
         one, two = SENDS[0][t], SENDS[1][t]
-        dx, dy, k, i = [
+        kinds = [k * (1 + (dx + dy) % 2) for dx, dy, k in (one, two)]
+        dx, dy, _, i = [
             choose(a, b) for a, b in zip(one + (INDEX[one],), two + (INDEX[two],))
         ]
+        kind = choose(*kinds)
         return pltpu.make_async_remote_copy(
             src_ref=send_ref.at[rows_of(i)],
             dst_ref=recv.at[c, rows_of(i)],
             send_sem=d_send.at[i],
             recv_sem=d_recv.at[i],
-            device_id=(at(dx, dy), c, jnp.where(k == 0, z, q)),
+            device_id=(at(dx, dy), c, jnp.where(kind == 0, z, jnp.where(kind == 1, q, p))),
             device_id_type=MESH,
         )
 
@@ -195,7 +207,7 @@
     for g in range(4):
         pack(g)
         if g == 0:
-            pl.semaphore_wait(barrier, 2 * PEERS + 1)
+            pl.semaphore_wait(barrier, 2 * PEERS + PEERS // 2 + 1)
             local.start()
         for t in range(g * GROUP, (g + 1) * GROUP):
             if SENDS[0][t] == (0, 0, 0):
@@ -276,6 +288,43 @@
             device_id_type=MESH,
         )
 
+    def to_next(ch, i):
+        return pltpu.make_async_remote_copy(
+            src_ref=sendp.at[i, ch, 0],
+            dst_ref=passing.at[i, ch],
+            send_sem=p_send.at[i, ch, 0],
+            recv_sem=n_recv.at[i, ch],
+            device_id=(at(1, 0), c, p),
+            device_id_type=MESH,
+        )
+
+    def from_next(ch, i):
+        return pltpu.make_async_remote_copy(
+            src_ref=passing.at[i, ch],
+            dst_ref=recvp.at[i, ch, 0],
+            send_sem=n_send.at[i, ch],
+            recv_sem=p_recv.at[i, ch, 0],
+            device_id=(at(3, 0), c, z),
+            device_id_type=MESH,
+        )
+
+    def hand_on(i):
+        def body(ch, _):
+            to_next(ch, i).wait_recv()
+            from_next(ch, i).start()
+            return 0
+
+        lax.fori_loop(0, DETOURS[i], body, 0)
+
+    def dispatch_slice(ch, m, i):
+        if m > 0 or DETOURS[i] == 0:
+            to_mate(ch, m, i).start()
+        elif DETOURS[i] == NCH:
+            to_next(ch, i).start()
+        else:
+            pl.when(ch < DETOURS[i])(lambda: to_next(ch, i).start())
+            pl.when(ch >= DETOURS[i])(lambda: to_mate(ch, m, i).start())
+
     def weight_grad(m, ch, part):
         lhs = turned[0 if m < 2 else 1, part]
         return jnp.dot(lhs, acts[m, ch], preferred_element_type=F32)
@@ -288,7 +337,7 @@
         lax.fori_loop(3, 4, rest, 0)
         for m in range(3):
             sendp[0, ch, m] = weight_grad(m, ch, o).astype(BF)
-            to_mate(ch, m, 0).start()
+            dispatch_slice(ch, m, 0)
         return 0
 
     lax.fori_loop(0, NCH, beyond, 0)
@@ -325,11 +374,12 @@
         return 0
 
     lax.fori_loop(0, 4, input_grad, 0)
+    hand_on(0)
 
     def ending(ch, _):
         for m in range(3):
             sendp[1, ch, m] = weight_grad(m, ch, p).astype(BF)
-            to_mate(ch, m, 1).start()
+            dispatch_slice(ch, m, 1)
         return 0
 
 
@@ -345,9 +395,11 @@
         )
 
     def take_back(s, k):
+        alike = lax.rem(s // 4 + lax.rem(s, 4), 2) == lax.rem(ex + ey, 2)
+        theirs = jnp.where(alike, own, own_flip)
         return pltpu.make_async_remote_copy(
             src_ref=ret.at[rows_of(0)],
-            dst_ref=back.at[s, own if k == 0 else 1 - own],
+            dst_ref=back.at[s, theirs if k == 0 else 1 - theirs],
             send_sem=r_send.at[0],
             recv_sem=r_recv.at[k, s],
             device_id=(s, c, plane[k]),
@@ -391,6 +443,7 @@
         return 0
 
     lax.fori_loop(0, NCH, pass_on, 0)
+    hand_on(1)
 
     def finish(ch, _):
         for m in range(3):
@@ -460,6 +513,14 @@
         return 0
 
     lax.fori_loop(0, NCH, drain, 0)
+
+    for i in range(2):
+
+        def drain_passing(ch, _, i=i):
+            from_next(ch, i).wait_send()
+            return 0
+
+        lax.fori_loop(0, DETOURS[i], drain_passing, 0)
 
 
 def layer(routes, levels, frames, out_grad, w_gate, w_up, w_down):
@@ -486,6 +547,7 @@
             pltpu.VMEM((3, NCH, ROWS, CH), BF),
             pltpu.VMEM((2, NCH, 3, SL, CH), BF),
             pltpu.VMEM((2, NCH, 3, SL, CH), BF),
+            pltpu.VMEM((2, NCH, SL, CH), BF),
             pltpu.VMEM((4, RB, HALF), F32),
             pltpu.VMEM((4, RB, HALF), BF),
             pltpu.VMEM((4, RB, HALF), BF),
@@ -503,6 +565,8 @@
             dma((NBLOCK,)),
             dma((2, NCH, 3)),
             dma((2, NCH, 3)),
+            dma((2, NCH)),
+            dma((2, NCH)),
             dma((4,)),
             dma((4,)),
             dma((NBLOCK,)),

time: 129 us -> 126 us (0.977)
  Pallas kernels: 129 us -> 125 us
    pallas_call x1, Pallas kernels: 126 us -> 123 us  [layer(): pl.pallas_call(layer_kernel, out_shape=[grad, grad, grad, jax.ShapeDtypeS...]
where the time goes in v3:
time: 126 us
  Pallas kernels  125 us (99%)
    pallas_call x1, Pallas kernels, layer(): pl.pallas_call(layer_kernel, out_shape=[grad, grad, grad, jax.ShapeDtypeS...  123 us
    pallas_call x1, Pallas kernels, settle(): pl.pallas_call(settle_kernel, out_shape=[jax.ShapeDtypeStruct(a.shape, a....  2.96 us

profile of v3, /device:TPU:1, one launch (start us, length us, event | category | flops | bytes accessed | tf_op | source)
XLA Modules:
  0.0 126.1 jit_solution(10287470312259855608)
XLA Ops:
  0.6 122.5 %layer.1 = (bf16[2,256,1024]{2,1,0:T(8,128)(2,1)}, bf16[2,256,1024]{2,1,0:T(8,128)(2,1)}, bf16[2,256,1024]{2,1,0:T(8,128)(2,1)}, bf16[384,512]{1,0:T(8,128)(2,1)}) custom-call(s32[2,384]{1,0:T(2,128)} %bitcast.2, s32[2,384]{1,0:T(2,128)} %bitcast.3, bf16[384,512]{1,0:T(8,128)(2,1)} %frames_hbm.1, bf16[384,512]{1,0:T(8,128)(2,1)} %grads_hbm.1, ...), custom_call_target="tpu_custom_call" | custom-call | flops 25769803776 | bytes 20000000 | tf_op jit(solution)/shard_map/layer/pallas_call | solution.py:529
  123.2 3.0 %settle.1 = (bf16[2,256,1024]{2,1,0:T(8,128)(2,1)}, bf16[2,256,1024]{2,1,0:T(8,128)(2,1)}, bf16[2,256,1024]{2,1,0:T(8,128)(2,1)}, bf16[384,512]{1,0:T(8,128)(2,1)}) custom-call(bf16[2,256,1024]{2,1,0:T(8,128)(2,1)} %get-tuple-element.12.refs_0_, bf16[2,256,1024]{2,1,0:T(8,128)(2,1)} %get-tuple-element.13.refs_1_, ...), custom_call_target="tpu_custom_call" | custom-call | tf_op jit(solution)/shard_map/settle/pallas_call | solution.py:616

commit v4 on v3

--- a/solution.py
+++ b/solution.py
@@ -268,14 +268,20 @@
 
         lax.fori_loop(0, 2, body, 0)
 
+    def turn_part(g, part):
+        rows = group_rows(g)
+        for t in range(2):
+            cols = pl.ds(pl.multiple_of(t * HALF + lax.rem(part, 2) * SL, SL), SL)
+            turned[t, part, :, rows] = recv[part // 2, rows, cols].T
+
     def early(i, _):
         forward(i // NCH, lax.rem(i, NCH))
         return 0
 
     for g in range(4):
         arrive(g)
-        turn(g)
         if g < 3:
+            turn(g)
             lax.fori_loop(g * NCH, (g + 1) * NCH, early, 0)
 
     def to_mate(ch, m, i):
@@ -335,12 +341,15 @@
             return 0
 
         lax.fori_loop(3, 4, rest, 0)
-        for m in range(3):
+        for m in (1, 0, 2):
             sendp[0, ch, m] = weight_grad(m, ch, o).astype(BF)
             dispatch_slice(ch, m, 0)
         return 0
 
+    turn_part(3, o)
     lax.fori_loop(0, NCH, beyond, 0)
+    for part in (p, q, z):
+        turn_part(3, part)
 
     def swap(b):
         return pltpu.make_async_remote_copy(
@@ -435,7 +444,7 @@
         return pltpu.make_async_copy(outs.at[ch, m], place_of(ch, m, own), o_sem.at[ch, m])
 
     def pass_on(ch, _):
-        for m in range(3):
+        for m in (1, 2, 0):
             total = weight_grad(m, ch, q)
             to_mate(ch, m, 0).wait_recv()
             outq[ch, m] = (total + recvp[0, ch, m].astype(F32)).astype(BF)
@@ -593,9 +602,9 @@
     in_sem, out_sem = refs[3 * n :]
     pieces = []
     for i in range(n):
-        half = ins[i].shape[0] // 2
-        for j in range(2):
-            part = pl.ds(j * half, half)
+        rows = ins[i].shape[-2] // (4 if ins[i].ndim == 2 else 2)
+        for j in range(4):
+            part = pl.ds(j * rows, rows) if ins[i].ndim == 2 else (j // 2, pl.ds(j % 2 * rows, rows))
             pieces.append(
                 (
                     pltpu.make_async_copy(ins[i].at[part], held[i].at[part], in_sem.at[i, j]),
@@ -619,7 +628,7 @@
         in_specs=[ANY] * n,
         out_specs=[ANY] * n,
         scratch_shapes=[pltpu.VMEM(a.shape, a.dtype) for a in arrays]
-        + [pltpu.SemaphoreType.DMA((n, 2))] * 2,
+        + [pltpu.SemaphoreType.DMA((n, 4))] * 2,
         name="settle",
     )(*arrays)
 

time: 126 us -> 126 us (level)
  no operation moved by 1% of the time
where the time goes in v4:
time: 126 us
  Pallas kernels  125 us (99%)
    pallas_call x1, Pallas kernels, layer(): pl.pallas_call(layer_kernel, out_shape=[grad, grad, grad, jax.ShapeDtypeS...  122 us
    pallas_call x1, Pallas kernels, settle(): pl.pallas_call(settle_kernel, out_shape=[jax.ShapeDtypeStruct(a.shape, a....  3.09 us

profile of v4, /device:TPU:1, one launch (start us, length us, event | category | flops | bytes accessed | tf_op | source)
XLA Modules:
  0.0 125.7 jit_solution(11860211252073638469)
XLA Ops:
  0.6 121.8 %layer.1 = (bf16[2,256,1024]{2,1,0:T(8,128)(2,1)}, bf16[2,256,1024]{2,1,0:T(8,128)(2,1)}, bf16[2,256,1024]{2,1,0:T(8,128)(2,1)}, bf16[384,512]{1,0:T(8,128)(2,1)}) custom-call(s32[2,384]{1,0:T(2,128)} %bitcast.2, s32[2,384]{1,0:T(2,128)} %bitcast.3, bf16[384,512]{1,0:T(8,128)(2,1)} %frames_hbm.1, bf16[384,512]{1,0:T(8,128)(2,1)} %grads_hbm.1, ...), custom_call_target="tpu_custom_call" | custom-call | flops 25769803776 | bytes 20000000 | tf_op jit(solution)/shard_map/layer/pallas_call | solution.py:538
  122.4 3.1 %settle.1 = (bf16[2,256,1024]{2,1,0:T(8,128)(2,1)}, bf16[2,256,1024]{2,1,0:T(8,128)(2,1)}, bf16[2,256,1024]{2,1,0:T(8,128)(2,1)}, bf16[384,512]{1,0:T(8,128)(2,1)}) custom-call(bf16[2,256,1024]{2,1,0:T(8,128)(2,1)} %get-tuple-element.12.refs_0_, bf16[2,256,1024]{2,1,0:T(8,128)(2,1)} %get-tuple-element.13.refs_1_, ...), custom_call_target="tpu_custom_call" | custom-call | tf_op jit(solution)/shard_map/settle/pallas_call | solution.py:625

commit v5 on v4

--- a/solution.py
+++ b/solution.py
@@ -341,7 +341,7 @@
             return 0
 
         lax.fori_loop(3, 4, rest, 0)
-        for m in (1, 0, 2):
+        for m in (1, 2, 0):
             sendp[0, ch, m] = weight_grad(m, ch, o).astype(BF)
             dispatch_slice(ch, m, 0)
         return 0

time: 126 us -> 126 us (level)
  no operation moved by 1% of the time
where the time goes in v5:
time: 126 us
  Pallas kernels  125 us (99%)
    pallas_call x1, Pallas kernels, layer(): pl.pallas_call(layer_kernel, out_shape=[grad, grad, grad, jax.ShapeDtypeS...  122 us
    pallas_call x1, Pallas kernels, settle(): pl.pallas_call(settle_kernel, out_shape=[jax.ShapeDtypeStruct(a.shape, a....  3.09 us

profile of v5, /device:TPU:1, one launch (start us, length us, event | category | flops | bytes accessed | tf_op | source)
XLA Modules:
  0.0 125.7 jit_solution(11032965685144942409)
XLA Ops:
  0.6 121.8 %layer.1 = (bf16[2,256,1024]{2,1,0:T(8,128)(2,1)}, bf16[2,256,1024]{2,1,0:T(8,128)(2,1)}, bf16[2,256,1024]{2,1,0:T(8,128)(2,1)}, bf16[384,512]{1,0:T(8,128)(2,1)}) custom-call(s32[2,384]{1,0:T(2,128)} %bitcast.2, s32[2,384]{1,0:T(2,128)} %bitcast.3, bf16[384,512]{1,0:T(8,128)(2,1)} %frames_hbm.1, bf16[384,512]{1,0:T(8,128)(2,1)} %grads_hbm.1, ...), custom_call_target="tpu_custom_call" | custom-call | flops 25769803776 | bytes 20000000 | tf_op jit(solution)/shard_map/layer/pallas_call | solution.py:538
  122.4 3.1 %settle.1 = (bf16[2,256,1024]{2,1,0:T(8,128)(2,1)}, bf16[2,256,1024]{2,1,0:T(8,128)(2,1)}, bf16[2,256,1024]{2,1,0:T(8,128)(2,1)}, bf16[384,512]{1,0:T(8,128)(2,1)}) custom-call(bf16[2,256,1024]{2,1,0:T(8,128)(2,1)} %get-tuple-element.12.refs_0_, bf16[2,256,1024]{2,1,0:T(8,128)(2,1)} %get-tuple-element.13.refs_1_, ...), custom_call_target="tpu_custom_call" | custom-call | tf_op jit(solution)/shard_map/settle/pallas_call | solution.py:625
